TPU v7x, 128 devices: a whole 4x4x4 slice. The times are simulated.
128 devices in a mesh: dp: 16 (over x, y), vocab: 8 (over z, core).
Axes of the slice: x: 4, y: 4, z: 4, core: 2. Of those that a mesh axis runs over, the one named last changes fastest.
Arguments:
- pol_hidden: bfloat16 [512, 8192], P(None, 'dp'), may hold values from -82 to 82
- pol_weight: bfloat16 [8192, 65536], P('dp', 'vocab'), may hold values from -0.0625 to 0.0625
- ref_logits: bfloat16 [256, 65536], P('dp', 'vocab'), may hold values from -205 to 205
- targets: int32 [256], replicated, may hold values from 0 to 65535
- owners: int32 [256, 1], replicated, may hold values from 0 to 15; in each aligned block of 16 rows (0 to 15, 16 to 31, ...) at most 2 rows name the same one
- grad_logprob: float32 [512], replicated, may hold values from -9 to 9
- grad_kl: float32 [512], replicated, may hold values from -96 to 96
Outputs:
- token_logprob: float32 [512], P('dp')
- token_kl: float32 [512], P('dp')
- normalizer: float32 [512], P('dp')
- feature_grad: bfloat16 [512, 8192], P('vocab', 'dp')
- weight_grad: bfloat16 [8192, 65536], P('dp', 'vocab')
Inputs may be any that keep to these rules, and one draw needn't show every extreme that they name: `owners`: in each aligned block of 16 rows (the rows of one device along dp) no owner is named more than 2 times, a bound that some block reaches.
All inputs are finite; a program needn't handle non-finite values.
Results may differ from a plain program's by a relative error of at most 0.015.
Values may be sent and summed in bfloat16 or wider, within the bound.
A program may use at most 128 MiB of HBM per device.

v0:
```python
import functools

import jax
import jax.numpy as jnp
from jax import lax
from jax.experimental import pallas as pl
from jax.experimental.pallas import tpu as pltpu
from jax.sharding import PartitionSpec as P

F32 = jnp.float32
BF16 = jnp.bfloat16
I32 = jnp.int32
MESH = pl.DeviceIdType.MESH
SIDE = 4
LANES = 128
GROUPS = 2
ROWS = 8
FLOWS = ((0, 1), (0, -1), (1, 1), (1, -1))
LARGEST = 32766.0


def encode(blocks, dst):
    tiles = blocks[0].shape[1] // (2 * LANES)
    parts = []
    for block in blocks:
        for t in range(tiles):
            u = t + tiles
            parts.append(
                (block[:, t * LANES : (t + 1) * LANES], block[:, u * LANES : (u + 1) * LANES])
            )
    peak = jnp.full((ROWS, LANES), 1e-30, F32)
    for high, low in parts:
        peak = jnp.maximum(peak, jnp.maximum(jnp.abs(high), jnp.abs(low)))
    power = jnp.ceil(jnp.log2(peak) * 8.0)
    inverse = jnp.exp2(power * -0.125) * LARGEST
    for k, (high, low) in enumerate(parts):
        high_code = jnp.round(high * inverse).astype(I32)
        low_code = jnp.round(low * inverse).astype(I32)
        dst[:, k * LANES : (k + 1) * LANES] = (high_code << 16) | (low_code & 0xFFFF)
    end = len(parts) * LANES
    dst[:, end : end + LANES] = power.astype(I32)


def decode(src, block, width):
    end = src.shape[1] - LANES
    scale = jnp.exp2(src[:, end : end + LANES].astype(F32) * 0.125) * (1.0 / LARGEST)
    highs, lows = [], []
    for t in range(width // (2 * LANES)):
        start = block * (width // 2) + t * LANES
        word = src[:, start : start + LANES]
        highs.append((word >> 16).astype(F32) * scale)
        lows.append(((word << 16) >> 16).astype(F32) * scale)
    return jnp.concatenate(highs + lows, axis=1)


def head_kernel(
    vocab_count,
    hidden_hbm,
    weight_hbm,
    ref_hbm,
    target_hbm,
    owner_hbm,
    cot_lp_hbm,
    cot_kl_hbm,
    grads_out,
    rows_out,
    feature_out,
    tokens_out,
    hidden,
    ref,
    target_row,
    owner_row,
    cot_lp,
    cot_kl,
    rows,
    rows_turned,
    feature_result,
    tokens_result,
    weight,
    part,
    send1,
    recv1,
    send2,
    recv2,
    logits,
    grads,
    peaks,
    cots,
    stats,
    tokens,
    slots,
    ref32,
    core_recv,
    zsend,
    zrecv,
    in_sem,
    w_sem,
    rs_send,
    rs_recv,
    ag_send,
    ag_recv,
    st_send,
    st_recv,
    tk_send,
    tk_recv,
    core_send_sem,
    core_recv_sem,
    z_send,
    z_recv,
    out_sem,
    end_sem,
):
    width = weight.shape[2]
    rows_all = hidden.shape[0]
    count = owner_row.shape[1]
    chips = SIDE * SIDE
    rows_dev = count // chips
    levels = vocab_count // 2
    dp = lax.axis_index("dp")
    vocab = lax.axis_index("vocab")
    here = (dp // SIDE, dp % SIDE)
    level, core = vocab // 2, vocab % 2

    def along(axis, offset):
        return lax.rem(here[axis] + offset + SIDE, SIDE)

    def device(axis, offset):
        moved = along(axis, offset)
        return (moved * SIDE + here[1], vocab) if axis == 0 else (here[0] * SIDE + moved, vocab)

    def place(f, first, second):
        return (first, second) if FLOWS[f][0] == 0 else (second, first)

    barrier = pltpu.get_barrier_semaphore()
    for axis in range(2):
        for step in range(1, SIDE):
            pl.semaphore_signal(barrier, inc=1, device_id=device(axis, step), device_id_type=MESH)
    for step in range(1, vocab_count):
        pl.semaphore_signal(
            barrier, inc=1, device_id=(dp, (vocab + step) % vocab_count), device_id_type=MESH
        )
    greeted = 2 * (SIDE - 1) + vocab_count - 1

    inputs = [
        pltpu.make_async_copy(source, landing, in_sem.at[k])
        for k, (source, landing) in enumerate(
            (
                (owner_hbm, owner_row),
                (hidden_hbm, hidden),
                (cot_lp_hbm, cot_lp),
                (cot_kl_hbm, cot_kl),
                (target_hbm, target_row),
                (ref_hbm, ref),
            )
        )
    ]
    for copy in inputs:
        copy.start()

    def weight_copy(f):
        cols = pl.ds(f * width, width)
        return pltpu.make_async_copy(weight_hbm.at[:, cols], weight.at[f], w_sem.at[f])

    for f in range(4):
        weight_copy(f).start()

    def iota(shape, dim):
        return lax.broadcasted_iota(I32, shape, dim)

    inputs[0].wait()
    rows_i, cols_i = iota((count, count), 0), iota((count, count), 1)
    diagonal = rows_i == cols_i

    def turned(row):
        return jnp.sum(jnp.where(diagonal, row, 0), axis=1, keepdims=True)

    owner_col = turned(owner_row[...].astype(F32)).astype(I32)
    alike = (owner_col == owner_row[...]) & (rows_i // rows_dev == cols_i // rows_dev)
    before_col = jnp.sum(jnp.where(alike & (cols_i < rows_i), 1.0, 0.0), axis=1, keepdims=True)
    before_row = jnp.sum(jnp.where(alike & (rows_i < cols_i), 1.0, 0.0), axis=0, keepdims=True)
    slot_count = rows_all // chips
    capacity = slot_count // chips
    slot_col = (
        owner_col * slot_count
        + (iota((count, 1), 0) // rows_dev) * capacity
        + before_col.astype(I32)
    )
    slot_row = (
        owner_row[...] * slot_count
        + (iota((1, count), 1) // rows_dev) * capacity
        + before_row.astype(I32)
    )
    placing = slot_col == iota((count, rows_all), 1)
    inputs[1].wait()
    rows[...] = jnp.dot(
        jnp.where(placing, 1.0, 0.0).astype(BF16), hidden[...], preferred_element_type=F32
    ).astype(BF16)

    def rs_copy(s, f, kind):
        axis, way = FLOWS[f]
        stage, role = kind // 3, kind % 3
        if stage == 1:
            axis = 1 - axis
        source, landing = (send1, recv1) if stage == 0 else (send2, recv2)
        return pltpu.make_async_remote_copy(
            src_ref=source.at[s, f, role],
            dst_ref=landing.at[s, f, role],
            send_sem=rs_send.at[s, stage],
            recv_sem=rs_recv.at[s, kind],
            device_id=device(axis, -way if role == 1 else way),
            device_id_type=MESH,
        )

    def rs_arrived(s, kind):
        landing = (recv1, recv2)[kind // 3].at[s, :, kind % 3]
        pltpu.make_async_copy(landing, landing, rs_recv.at[s, kind]).wait()

    def first_blocks(s, f, offset):
        first = along(FLOWS[f][0], offset)
        return [part[(s, f) + place(f, first, k)] for k in range(SIDE)]

    def second_block(s, f, offset):
        axis = FLOWS[f][0]
        return part[(s, f) + place(f, here[axis], along(1 - axis, offset))]

    def multiply(f):
        weight_copy(f).wait()
        product = jnp.dot(rows[...], weight[f], preferred_element_type=F32)
        product = product.reshape(SIDE, SIDE, rows_dev, width)
        part[0, f] = product[:, :, 0:ROWS]
        part[1, f] = product[:, :, ROWS:rows_dev]

    def first_ahead(s, f):
        encode(first_blocks(s, f, 2), send1.at[s, f, 0])
        rs_copy(s, f, 0).start()

    def first_back(s, f):
        encode(first_blocks(s, f, -FLOWS[f][1]), send1.at[s, f, 1])
        rs_copy(s, f, 1).start()

    def first_relay(s):
        rs_arrived(s, 0)
        for f in range(4):
            own = first_blocks(s, f, FLOWS[f][1])
            arrived = recv1.at[s, f, 0]
            encode(
                [own[k] + decode(arrived, k, width) for k in range(SIDE)], send1.at[s, f, 2]
            )
        for f in range(4):
            rs_copy(s, f, 2).start()

    def first_sum(s):
        rs_arrived(s, 1)
        rs_arrived(s, 2)
        for f in range(4):
            axis, way = FLOWS[f]
            for k in range(SIDE):
                spot = (s, f) + place(f, here[axis], k)
                part[spot] = (
                    part[spot]
                    + decode(recv1.at[s, f, 1], k, width)
                    + decode(recv1.at[s, f, 2], k, width)
                )
        for f in range(4):
            way = FLOWS[f][1]
            encode([second_block(s, f, 2)], send2.at[s, f, 0])
            encode([second_block(s, f, -way)], send2.at[s, f, 1])
        for f in range(4):
            rs_copy(s, f, 3).start()
            rs_copy(s, f, 4).start()

    def second_relay(s):
        rs_arrived(s, 3)
        for f in range(4):
            encode(
                [second_block(s, f, FLOWS[f][1]) + decode(recv2.at[s, f, 0], 0, width)],
                send2.at[s, f, 2],
            )
        for f in range(4):
            rs_copy(s, f, 5).start()

    def second_sum(s):
        rs_arrived(s, 4)
        rs_arrived(s, 5)
        peak = jnp.full((ROWS, LANES), -jnp.inf, F32)
        for f in range(4):
            done = (
                second_block(s, f, 0)
                + decode(recv2.at[s, f, 1], 0, width)
                + decode(recv2.at[s, f, 2], 0, width)
            )
            logits[s, f] = done
            for t in range(width // LANES):
                peak = jnp.maximum(peak, done[:, t * LANES : (t + 1) * LANES])
        peaks[s] = peak

    def ref_piece(s, f):
        return ref32[s * ROWS : (s + 1) * ROWS, f * width : (f + 1) * width]

    def lane_sum(values):
        total = values[:, 0:LANES]
        for t in range(1, width // LANES):
            total = total + values[:, t * LANES : (t + 1) * LANES]
        return total

    first_col = vocab * (4 * width)
    lane = iota((ROWS, LANES), 1)

    def my_cots(s):
        start = pl.multiple_of(dp * rows_dev, rows_dev) + s * ROWS
        mine = cots[pl.ds(pl.multiple_of(start, ROWS), ROWS), :]
        return mine[:, 0:1], mine[:, 1:2], mine[:, 2:3].astype(I32)

    def hit(f, target):
        return first_col + f * width + iota((ROWS, width), 1) == target

    def ref_stats(s):
        peak = jnp.full((ROWS, 1), -jnp.inf, F32)
        for f in range(4):
            peak = jnp.maximum(peak, jnp.max(ref_piece(s, f), axis=1, keepdims=True))
        mass = jnp.zeros((ROWS, LANES), F32)
        for f in range(4):
            mass = mass + lane_sum(jnp.exp(ref_piece(s, f) - peak))
        return peak, jnp.sum(mass, axis=1, keepdims=True)

    def stats_copy(s, step):
        return pltpu.make_async_remote_copy(
            src_ref=stats.at[s, vocab],
            dst_ref=stats.at[s, vocab],
            send_sem=st_send.at[s],
            recv_sem=st_recv.at[s],
            device_id=(dp, (vocab + step) % vocab_count),
            device_id_type=MESH,
        )

    def stats_send(s, ref_side):
        target = my_cots(s)[2]
        peak = jnp.max(peaks[s], axis=1, keepdims=True)
        mass = cross = picked = jnp.zeros((ROWS, LANES), F32)
        for f in range(4):
            values = logits[s, f]
            weights = jnp.exp(values - peak)
            mass = mass + lane_sum(weights)
            cross = cross + lane_sum(weights * (values - ref_piece(s, f)))
            picked = picked + lane_sum(jnp.where(hit(f, target), values, 0.0))
        mass, cross, picked = [
            jnp.sum(value, axis=1, keepdims=True) for value in (mass, cross, picked)
        ]
        packed = jnp.zeros((ROWS, LANES), F32)
        for k, value in enumerate((peak, mass, cross) + ref_side + (picked,)):
            packed = packed + jnp.where(lane == k, value, 0.0)
        stats[s, vocab] = packed
        for step in range(1, vocab_count):
            stats_copy(s, step).start()

    def other_stats(s):
        return stats.at[s, pl.ds(0, vocab_count - 1)]

    def stats_finish(s):
        pltpu.make_async_copy(other_stats(s), other_stats(s), st_recv.at[s]).wait()
        every = [stats[s, k] for k in range(vocab_count)]
        peak, ref_peak = every[0][:, 0:1], every[0][:, 3:4]
        for tile in every[1:]:
            peak = jnp.maximum(peak, tile[:, 0:1])
            ref_peak = jnp.maximum(ref_peak, tile[:, 3:4])
        mass, cross, ref_mass, picked = 0.0, 0.0, 0.0, 0.0
        for tile in every:
            scale = jnp.exp(tile[:, 0:1] - peak)
            mass = mass + tile[:, 1:2] * scale
            cross = cross + tile[:, 2:3] * scale
            ref_mass = ref_mass + tile[:, 4:5] * jnp.exp(tile[:, 3:4] - ref_peak)
            picked = picked + tile[:, 5:6]
        norm = peak + jnp.log(mass)
        ref_norm = ref_peak + jnp.log(ref_mass)
        row_kl = cross / mass - norm + ref_norm
        tokens[here[0], here[1], s * ROWS : (s + 1) * ROWS] = (
            jnp.where(lane == 0, picked - norm, 0.0)
            + jnp.where(lane == 1, row_kl, 0.0)
            + jnp.where(lane == 2, norm, 0.0)
        )
        return norm, ref_norm - norm - row_kl

    half = width // 2

    def gradients(s, norm, shift):
        lp, kl, target = my_cots(s)
        for f in range(4):
            values = logits[s, f]
            probs = jnp.exp(values - norm)
            excess = values - ref_piece(s, f) + shift
            result = jnp.where(hit(f, target), lp, 0.0) + probs * (kl * excess - lp)
            result = jnp.concatenate([result[:, 0:half], result[:, half:width]], axis=0)
            grads[s, f, here[0], here[1]] = result.astype(BF16)

    def relay_copy(buffer, f, kind, send_sem, recv_sem):
        axis, way = FLOWS[f]
        other = 1 - axis
        if kind < 3:
            spot = place(f, along(axis, -way if kind == 2 else 0), here[other])
            to = device(axis, -way if kind == 1 else way)
        else:
            spot = place(f, slice(None), along(other, -way if kind == 5 else 0))
            to = device(other, -way if kind == 4 else way)
        block = buffer.at[spot]
        return pltpu.make_async_remote_copy(
            src_ref=block,
            dst_ref=block,
            send_sem=send_sem,
            recv_sem=recv_sem,
            device_id=to,
            device_id_type=MESH,
        )

    def ag_copy(g, f, kind):
        return relay_copy(grads.at[g, f], f, kind, ag_send.at[g, kind // 3], ag_recv.at[g, kind])

    def ag_go(g, kinds):
        for kind in kinds:
            for f in range(4):
                ag_copy(g, f, kind).start()

    def ag_arrived(g, kinds):
        for kind in kinds:
            landing = grads.at[g, 0] if kind >= 3 else grads.at[g, 0, 0]
            pltpu.make_async_copy(landing, landing, ag_recv.at[g, kind]).wait()

    def tokens_copy(axis, step):
        block = tokens.at[here] if axis == 1 else tokens.at[here[0]]
        return pltpu.make_async_remote_copy(
            src_ref=block,
            dst_ref=block,
            send_sem=tk_send.at[axis],
            recv_sem=tk_recv.at[axis],
            device_id=device(axis, step),
            device_id_type=MESH,
        )

    def tokens_go(axis):
        for step in range(1, SIDE):
            tokens_copy(axis, step).start()

    def tokens_moved(axis, sem):
        moved = tokens.at[0, pl.ds(0, 3)] if axis == 1 else tokens.at[pl.ds(0, 3)]
        pltpu.make_async_copy(moved, moved, sem.at[axis]).wait()

    def out_copy(g, f):
        return pltpu.make_async_copy(grads.at[g, f], grads_out.at[g, f], out_sem.at[g, f])

    def group_token(g, shape, dim):
        order = iota(shape, dim)
        return (order // ROWS) * rows_dev + g * ROWS + lax.rem(order, ROWS)

    members = count // GROUPS

    def spread(g):
        shape = (count, members)
        chosen = iota(shape, 0) == group_token(g, shape, 1)
        slot_of = jnp.sum(jnp.where(chosen, slot_col.astype(F32), 0.0), axis=0, keepdims=True)
        matches = iota((rows_all, members), 0) == slot_of.astype(I32)
        return jnp.where(matches, 1.0, 0.0).astype(BF16)

    def feature_step(g):
        for f in range(4):
            out_copy(g, f).start()
        total = jnp.zeros((members, rows.shape[1]), F32)
        for f in range(4):
            for h in range(2):
                piece = grads[g, f, :, :, h * ROWS : (h + 1) * ROWS, :].reshape(members, half)
                total = total + lax.dot_general(
                    piece,
                    weight[f, :, h * half : (h + 1) * half],
                    (((1,), (1,)), ((), ())),
                    preferred_element_type=F32,
                )
        to_slots = spread(g)
        high = total.astype(BF16)
        rest = total - high.astype(F32)
        middle = rest.astype(BF16)
        low = (rest - middle.astype(F32)).astype(BF16)
        placed = jnp.dot(to_slots, high, preferred_element_type=F32)
        placed = placed + jnp.dot(to_slots, middle, preferred_element_type=F32)
        placed = placed + jnp.dot(to_slots, low, preferred_element_type=F32)
        return placed.reshape(slots.shape)

    for f in range(4):
        multiply(f)
        if f == 0:
            pl.semaphore_wait(barrier, greeted)
        first_ahead(0, f)
    for f in range(4):
        first_back(0, f)
    for copy in inputs[2:]:
        copy.wait()
    ref32[...] = ref[...].astype(F32)
    lp_col = jnp.sum(jnp.where(placing, cot_lp[...], 0.0), axis=1, keepdims=True)
    kl_col = jnp.sum(jnp.where(placing, cot_kl[...], 0.0), axis=1, keepdims=True)
    target_col = turned(target_row[...].astype(F32))
    lane_all = iota((count, LANES), 1)
    cots[...] = (
        jnp.where(lane_all == 0, lp_col, 0.0)
        + jnp.where(lane_all == 1, kl_col, 0.0)
        + jnp.where(lane_all == 2, target_col, 0.0)
    )
    first_relay(0)
    for f in range(4):
        first_ahead(1, f)
    for f in range(4):
        first_back(1, f)
    ref_side = [ref_stats(0), ref_stats(1)]
    for g in range(GROUPS):
        rows_turned[:, g * members : (g + 1) * members] = lax.dot_general(
            hidden[...], spread(g), (((0,), (0,)), ((), ())), preferred_element_type=F32
        ).astype(BF16)
    rows_copy = pltpu.make_async_copy(rows_turned, rows_out, end_sem.at[0])
    rows_copy.start()
    first_sum(0)
    first_relay(1)
    second_relay(0)
    first_sum(1)
    second_sum(0)
    stats_send(0, ref_side[0])
    second_relay(1)
    gradients(0, *stats_finish(0))
    ag_go(0, (0, 1))
    second_sum(1)
    stats_send(1, ref_side[1])
    ag_arrived(0, (0,))
    ag_go(0, (2,))
    gradients(1, *stats_finish(1))
    ag_go(1, (0, 1))
    tokens_go(1)
    ag_arrived(0, (1, 2))
    ag_go(0, (3, 4))
    ag_arrived(1, (0,))
    ag_go(1, (2,))
    ag_arrived(1, (1, 2))
    ag_go(1, (3, 4))
    ag_arrived(0, (3,))
    ag_go(0, (5,))
    ag_arrived(1, (3,))
    ag_go(1, (5,))
    tokens_moved(1, tk_recv)
    tokens_go(0)
    ag_arrived(0, (4, 5))
    slots[...] = feature_step(0)
    ag_arrived(1, (4, 5))
    slots[...] = slots[...] + feature_step(1)

    core_copy = pltpu.make_async_remote_copy(
        src_ref=slots.at[:, 1 - core],
        dst_ref=core_recv,
        send_sem=core_send_sem,
        recv_sem=core_recv_sem,
        device_id=(dp, level * 2 + 1 - core),
        device_id_type=MESH,
    )
    core_copy.start()

    tokens_moved(0, tk_recv)
    everyone = tokens[...].reshape(count, LANES)
    mine_slots = slot_col == dp * slot_count + lane_all
    mine_slots = mine_slots & (lane_all < slot_count)
    for k in range(3):
        tokens_result[k : k + 1, :] = jnp.sum(
            jnp.where(mine_slots, everyone[:, k : k + 1], 0.0), axis=0, keepdims=True
        )

    tokens_copied = pltpu.make_async_copy(tokens_result, tokens_out, end_sem.at[1])
    tokens_copied.start()
    core_copy.wait_recv()
    slot_rows = slots.shape[2]
    feature_width = slots.shape[3]

    def pair_sum(l):
        return slots[l, core] + core_recv[l]

    def z_copy(step):
        return pltpu.make_async_remote_copy(
            src_ref=zsend.at[step],
            dst_ref=zrecv.at[step],
            send_sem=z_send.at[step],
            recv_sem=z_recv.at[step],
            device_id=(dp, ((level + step) % levels) * 2 + core),
            device_id_type=MESH,
        )

    for step in (2, 1, 3):
        if step < levels:
            both = pair_sum((level + step) % levels)
            encode([both[k : k + ROWS] for k in range(0, slot_rows, ROWS)], zsend.at[step])
            z_copy(step).start()
    total = pair_sum(level)
    for step in range(1, levels):
        z_copy(step).wait_recv()
    pieces_out = []
    for k in range(slot_rows // ROWS):
        block = total[k * ROWS : (k + 1) * ROWS]
        for step in range(1, levels):
            block = block + decode(zrecv.at[step], k, feature_width)
        pieces_out.append(block)
    feature_result[...] = jnp.concatenate(pieces_out, axis=0).astype(BF16)
    feature_copied = pltpu.make_async_copy(feature_result, feature_out, end_sem.at[2])
    feature_copied.start()

    def left(source, sem):
        pltpu.make_async_copy(source, source, sem).wait()

    for s in range(GROUPS):
        left(send1.at[s], rs_send.at[s, 0])
        left(send2.at[s], rs_send.at[s, 1])
    for g in range(GROUPS):
        left(grads.at[g, :, 0, pl.ds(0, 3)], ag_send.at[g, 0])
        left(grads.at[g, pl.ds(0, 3)], ag_send.at[g, 1])
        for f in range(4):
            out_copy(g, f).wait()
        left(other_stats(g), st_send.at[g])
    for axis in range(2):
        tokens_moved(axis, tk_send)
    core_copy.wait_send()
    for step in range(1, levels):
        z_copy(step).wait_send()
    rows_copy.wait()
    tokens_copied.wait()
    feature_copied.wait()


def weight_kernel(
    rows_in,
    grads_in,
    feature_in,
    tokens_in,
    out,
    feature_out,
    first,
    second,
    third,
    rows,
    grads,
    tokens,
    small,
    result,
    in_sem,
    out_sem,
):
    width = grads.shape[5]
    members = rows.shape[1] // GROUPS

    def load(f):
        return pltpu.make_async_copy(grads_in.at[:, f], grads.at[f], in_sem.at[f])

    def store(f, h):
        cols = pl.ds((2 * f + h) * width, width)
        return pltpu.make_async_copy(result.at[f, h], out.at[:, cols], out_sem.at[f, h])

    rows_copy = pltpu.make_async_copy(rows_in, rows, in_sem.at[4])
    rows_copy.start()
    for f in range(4):
        load(f).start()
    tokens_copy = pltpu.make_async_copy(tokens_in, tokens, in_sem.at[5])
    tokens_copy.start()
    feature_copy = pltpu.make_async_copy(feature_in, feature_out, in_sem.at[6])
    feature_copy.start()
    rows_copy.wait()
    for f in range(4):
        load(f).wait()
        for h in range(2):
            total = 0.0
            for g in range(GROUPS):
                piece = grads[f, g, :, :, h * ROWS : (h + 1) * ROWS, :].reshape(members, width)
                total = total + jnp.dot(
                    rows[:, g * members : (g + 1) * members], piece, preferred_element_type=F32
                )
            result[f, h] = total.astype(BF16)
            store(f, h).start()
    tokens_copy.wait()
    outs = []
    for k, token_out in enumerate((first, second, third)):
        small[k] = tokens[k : k + 1, 0 : small.shape[2]]
        outs.append(pltpu.make_async_copy(small.at[k], token_out, in_sem.at[7 + k]))
        outs[-1].start()
    feature_copy.wait()
    for copy in outs:
        copy.wait()
    for f in range(4):
        for h in range(2):
            store(f, h).wait()


def per_device(
    vocab_count, pol_hidden, pol_weight, ref_logits, targets, owners, grad_logprob, grad_kl
):
    all_slots, depth = pol_hidden.shape
    cols = pol_weight.shape[1]
    rows_dev = ref_logits.shape[0]
    count = owners.shape[0]
    chips = SIDE * SIDE
    width = cols // 4
    slot_count = all_slots // chips
    levels = vocab_count // 2
    slot_rows = all_slots // vocab_count
    unit1 = (GROUPS, 4, 3, ROWS, SIDE * width // 2 + LANES)
    unit2 = (GROUPS, 4, 3, ROWS, width // 2 + LANES)
    unit3 = (levels, ROWS, slot_rows // ROWS * depth // 2 + LANES)
    grads_shape = (GROUPS, 4, SIDE, SIDE, rows_dev, width // 2)
    anywhere = pl.BlockSpec(memory_space=pl.ANY)
    flops = 2 * count * depth * cols * 2
    grads, rows, feature, tokens = pl.pallas_call(
        functools.partial(head_kernel, vocab_count),
        out_shape=(
            jax.ShapeDtypeStruct(grads_shape, BF16),
            jax.ShapeDtypeStruct((depth, count), BF16),
            jax.ShapeDtypeStruct((slot_rows, depth), BF16),
            jax.ShapeDtypeStruct((8, LANES), F32),
        ),
        in_specs=[pl.BlockSpec(memory_space=pltpu.HBM)] * 7,
        out_specs=(anywhere,) * 4,
        scratch_shapes=[
            pltpu.VMEM((all_slots, depth), BF16),
            pltpu.VMEM((rows_dev, cols), BF16),
            pltpu.VMEM((1, count), I32),
            pltpu.VMEM((1, count), I32),
            pltpu.VMEM((1, all_slots), F32),
            pltpu.VMEM((1, all_slots), F32),
            pltpu.VMEM((count, depth), BF16),
            pltpu.VMEM((depth, count), BF16),
            pltpu.VMEM((slot_rows, depth), BF16),
            pltpu.VMEM((8, LANES), F32),
            pltpu.VMEM((4, depth, width), BF16),
            pltpu.VMEM((GROUPS, 4, SIDE, SIDE, ROWS, width), F32),
            pltpu.VMEM(unit1, I32),
            pltpu.VMEM(unit1, I32),
            pltpu.VMEM(unit2, I32),
            pltpu.VMEM(unit2, I32),
            pltpu.VMEM((GROUPS, 4, ROWS, width), F32),
            pltpu.VMEM(grads_shape, BF16),
            pltpu.VMEM((GROUPS, ROWS, LANES), F32),
            pltpu.VMEM((count, LANES), F32),
            pltpu.VMEM((GROUPS, vocab_count, ROWS, LANES), F32),
            pltpu.VMEM((SIDE, SIDE, rows_dev, LANES), F32),
            pltpu.VMEM((levels, 2, slot_rows, depth), F32),
            pltpu.VMEM((rows_dev, cols), F32),
            pltpu.VMEM((levels, slot_rows, depth), F32),
            pltpu.VMEM(unit3, I32),
            pltpu.VMEM(unit3, I32),
            pltpu.SemaphoreType.DMA((6,)),
            pltpu.SemaphoreType.DMA((4,)),
            pltpu.SemaphoreType.DMA((GROUPS, 2)),
            pltpu.SemaphoreType.DMA((GROUPS, 6)),
            pltpu.SemaphoreType.DMA((GROUPS, 2)),
            pltpu.SemaphoreType.DMA((GROUPS, 6)),
            pltpu.SemaphoreType.DMA((GROUPS,)),
            pltpu.SemaphoreType.DMA((GROUPS,)),
            pltpu.SemaphoreType.DMA((2,)),
            pltpu.SemaphoreType.DMA((2,)),
            pltpu.SemaphoreType.DMA,
            pltpu.SemaphoreType.DMA,
            pltpu.SemaphoreType.DMA((levels,)),
            pltpu.SemaphoreType.DMA((levels,)),
            pltpu.SemaphoreType.DMA((GROUPS, 4)),
            pltpu.SemaphoreType.DMA((3,)),
        ],
        compiler_params=pltpu.CompilerParams(
            collective_id=0, has_side_effects=True, vmem_limit_bytes=60 * 2**20
        ),
        cost_estimate=pl.CostEstimate(
            flops=flops, bytes_accessed=3 * depth * cols, transcendentals=3 * rows_dev * cols
        ),
        name="head",
    )(
        pol_hidden,
        pol_weight,
        ref_logits,
        targets.reshape(1, count),
        owners.reshape(1, count),
        grad_logprob.reshape(1, all_slots),
        grad_kl.reshape(1, all_slots),
    )
    token_shape = jax.ShapeDtypeStruct((1, slot_count), F32)
    weight_grad, feature, first, second, third = pl.pallas_call(
        weight_kernel,
        out_shape=(
            jax.ShapeDtypeStruct((depth, cols), BF16),
            jax.ShapeDtypeStruct((slot_rows, depth), BF16),
            token_shape,
            token_shape,
            token_shape,
        ),
        in_specs=[anywhere] * 4,
        out_specs=(anywhere,) * 5,
        scratch_shapes=[
            pltpu.VMEM((depth, count), BF16),
            pltpu.VMEM((4, GROUPS) + grads_shape[2:], BF16),
            pltpu.VMEM((8, LANES), F32),
            pltpu.VMEM((3, 1, slot_count), F32),
            pltpu.VMEM((4, 2, depth, width // 2), BF16),
            pltpu.SemaphoreType.DMA((10,)),
            pltpu.SemaphoreType.DMA((4, 2)),
        ],
        compiler_params=pltpu.CompilerParams(vmem_limit_bytes=60 * 2**20),
        cost_estimate=pl.CostEstimate(
            flops=2 * count * depth * cols,
            bytes_accessed=2 * (depth + count) * cols,
            transcendentals=0,
        ),
        name="weight_grad",
    )(rows, grads, feature, tokens)
    return (
        first.reshape(slot_count),
        second.reshape(slot_count),
        third.reshape(slot_count),
        feature,
        weight_grad,
    )


def solution(mesh):
    in_specs = (P(None, "dp"), P("dp", "vocab"), P("dp", "vocab"), P(), P(), P(), P())
    out_specs = (P("dp"), P("dp"), P("dp"), P("vocab", "dp"), P("dp", "vocab"))
    return jax.shard_map(
        functools.partial(per_device, mesh.shape["vocab"]),
        mesh=mesh,
        in_specs=in_specs,
        out_specs=out_specs,
        check_vma=False,
    )
```

profile of v0, /device:TPU:1, one launch (start us, length us, event | category | flops | bytes accessed | tf_op | source)
XLA Modules:
  0.0 88.2 jit_solution(9209585738325419245)
XLA Ops:
  0.6 79.9 %head.1 = (bf16[2,4,4,4,16,1024]{5,4,3,2,1,0:T(8,128)(2,1)}, bf16[512,256]{1,0:T(8,128)(2,1)}, bf16[64,512]{1,0:T(8,128)(2,1)}, f32[8,128]{1,0:T(8,128)}) custom-call(bf16[512,512]{1,0:T(8,128)(2,1)} %hidden_hbm.1, bf16[512,8192]{1,0:T(8,128)(2,1)} %weight_hbm.1, bf16[16,8192]{1,0:T(8,128)(2,1)} %ref_hbm.1, s32[1,256]{1,0:T(1,128)} %bitcast.9, ...), custom_call_target="tpu_custom_call" | custom-call | flops 4294967296 | bytes 12582912 | tf_op jit(solution)/shard_map/head/pallas_call | solution.py:707
  80.5 7.5 %weight_grad.1 = (bf16[512,8192]{1,0:T(8,128)(2,1)}, bf16[64,512]{1,0:T(8,128)(2,1)}, f32[1,32]{1,0:T(1,128)}, f32[1,32]{1,0:T(1,128)}, f32[1,32]{1,0:T(1,128)}) custom-call(bf16[512,256]{1,0:T(8,128)(2,1)} %get-tuple-element.14.rows_in, bf16[2,4,4,4,16,1024]{5,4,3,2,1,0:T(8,128)(2,1)} %get-tuple-element.15.grads_in, ...), custom_call_target="tpu_custom_call" | custom-call | flops 2147483648 | bytes 12582912 | tf_op jit(solution)/shard_map/weight_grad/pallas_call | solution.py:779
where the time goes:
time: 88.3 us; the launch traced here: 88.2 us
  Pallas kernels  87.4 us (99%)
    pallas_call x1, Pallas kernels, per_device(): pl.pallas_call(functools.partial(head_kernel, vocab_count), out_shape=(ja...  79.9 us
    pallas_call x1, Pallas kernels, per_device(): pl.pallas_call(weight_kernel, out_shape=(jax.ShapeDtypeStruct((depth, col...  7.55 us

commit v1 on v0

--- a/solution.py
+++ b/solution.py
@@ -16,6 +16,7 @@
 GROUPS = 2
 ROWS = 8
 FLOWS = ((0, 1), (0, -1), (1, 1), (1, -1))
+ORDER = (0, 2, 1, 3)
 LARGEST = 32766.0
 
 
@@ -206,14 +207,10 @@
             src_ref=source.at[s, f, role],
             dst_ref=landing.at[s, f, role],
             send_sem=rs_send.at[s, stage],
-            recv_sem=rs_recv.at[s, kind],
-            device_id=device(axis, -way if role == 1 else way),
+            recv_sem=rs_recv.at[s, kind, f],
+            device_id=device(axis, 2 if kind == 3 else -way if role == 1 else way),
             device_id_type=MESH,
         )
-
-    def rs_arrived(s, kind):
-        landing = (recv1, recv2)[kind // 3].at[s, :, kind % 3]
-        pltpu.make_async_copy(landing, landing, rs_recv.at[s, kind]).wait()
 
     def first_blocks(s, f, offset):
         first = along(FLOWS[f][0], offset)
@@ -239,20 +236,19 @@
         rs_copy(s, f, 1).start()
 
     def first_relay(s):
-        rs_arrived(s, 0)
-        for f in range(4):
+        for f in ORDER:
+            rs_copy(s, f, 0).wait_recv()
             own = first_blocks(s, f, FLOWS[f][1])
             arrived = recv1.at[s, f, 0]
             encode(
                 [own[k] + decode(arrived, k, width) for k in range(SIDE)], send1.at[s, f, 2]
             )
-        for f in range(4):
             rs_copy(s, f, 2).start()
 
     def first_sum(s):
-        rs_arrived(s, 1)
-        rs_arrived(s, 2)
-        for f in range(4):
+        for f in ORDER:
+            rs_copy(s, f, 1).wait_recv()
+            rs_copy(s, f, 2).wait_recv()
             axis, way = FLOWS[f]
             for k in range(SIDE):
                 spot = (s, f) + place(f, here[axis], k)
@@ -261,31 +257,18 @@
                     + decode(recv1.at[s, f, 1], k, width)
                     + decode(recv1.at[s, f, 2], k, width)
                 )
-        for f in range(4):
-            way = FLOWS[f][1]
-            encode([second_block(s, f, 2)], send2.at[s, f, 0])
-            encode([second_block(s, f, -way)], send2.at[s, f, 1])
-        for f in range(4):
-            rs_copy(s, f, 3).start()
-            rs_copy(s, f, 4).start()
-
-    def second_relay(s):
-        rs_arrived(s, 3)
-        for f in range(4):
-            encode(
-                [second_block(s, f, FLOWS[f][1]) + decode(recv2.at[s, f, 0], 0, width)],
-                send2.at[s, f, 2],
-            )
-        for f in range(4):
-            rs_copy(s, f, 5).start()
+            for role, offset in ((0, 2), (1, -way), (2, way)):
+                encode([second_block(s, f, offset)], send2.at[s, f, role])
+                rs_copy(s, f, 3 + role).start()
 
     def second_sum(s):
-        rs_arrived(s, 4)
-        rs_arrived(s, 5)
         peak = jnp.full((ROWS, LANES), -jnp.inf, F32)
-        for f in range(4):
+        for f in ORDER:
+            for kind in (3, 4, 5):
+                rs_copy(s, f, kind).wait_recv()
             done = (
                 second_block(s, f, 0)
+                + decode(recv2.at[s, f, 0], 0, width)
                 + decode(recv2.at[s, f, 1], 0, width)
                 + decode(recv2.at[s, f, 2], 0, width)
             )
@@ -384,20 +367,23 @@
 
     def gradients(s, norm, shift):
         lp, kl, target = my_cots(s)
-        for f in range(4):
+        for f in ORDER:
             values = logits[s, f]
             probs = jnp.exp(values - norm)
             excess = values - ref_piece(s, f) + shift
             result = jnp.where(hit(f, target), lp, 0.0) + probs * (kl * excess - lp)
             result = jnp.concatenate([result[:, 0:half], result[:, half:width]], axis=0)
             grads[s, f, here[0], here[1]] = result.astype(BF16)
-
-    def relay_copy(buffer, f, kind, send_sem, recv_sem):
+            for kind in (0, 1, 2):
+                ag_copy(s, f, kind).start()
+
+    def relay_copy(buffer, f, kind, straight, send_sem, recv_sem):
         axis, way = FLOWS[f]
         other = 1 - axis
         if kind < 3:
-            spot = place(f, along(axis, -way if kind == 2 else 0), here[other])
-            to = device(axis, -way if kind == 1 else way)
+            relayed = kind == 2 and not straight
+            spot = place(f, along(axis, -way if relayed else 0), here[other])
+            to = device(axis, 2 if kind == 2 and straight else -way if kind == 1 else way)
         else:
             spot = place(f, slice(None), along(other, -way if kind == 5 else 0))
             to = device(other, -way if kind == 4 else way)
@@ -412,17 +398,16 @@
         )
 
     def ag_copy(g, f, kind):
-        return relay_copy(grads.at[g, f], f, kind, ag_send.at[g, kind // 3], ag_recv.at[g, kind])
-
-    def ag_go(g, kinds):
-        for kind in kinds:
-            for f in range(4):
+        return relay_copy(
+            grads.at[g, f], f, kind, True, ag_send.at[g, kind // 3], ag_recv.at[g, kind, f]
+        )
+
+    def ag_pass(g, waits, kinds):
+        for f in ORDER:
+            for kind in waits:
+                ag_copy(g, f, kind).wait_recv()
+            for kind in kinds:
                 ag_copy(g, f, kind).start()
-
-    def ag_arrived(g, kinds):
-        for kind in kinds:
-            landing = grads.at[g, 0] if kind >= 3 else grads.at[g, 0, 0]
-            pltpu.make_async_copy(landing, landing, ag_recv.at[g, kind]).wait()
 
     def tokens_copy(axis, step):
         block = tokens.at[here] if axis == 1 else tokens.at[here[0]]
@@ -460,10 +445,11 @@
         return jnp.where(matches, 1.0, 0.0).astype(BF16)
 
     def feature_step(g):
-        for f in range(4):
+        total = jnp.zeros((members, rows.shape[1]), F32)
+        for f in ORDER:
+            ag_copy(g, f, 4).wait_recv()
+            ag_copy(g, f, 5).wait_recv()
             out_copy(g, f).start()
-        total = jnp.zeros((members, rows.shape[1]), F32)
-        for f in range(4):
             for h in range(2):
                 piece = grads[g, f, :, :, h * ROWS : (h + 1) * ROWS, :].reshape(members, half)
                 total = total + lax.dot_general(
@@ -482,13 +468,15 @@
         placed = placed + jnp.dot(to_slots, low, preferred_element_type=F32)
         return placed.reshape(slots.shape)
 
-    for f in range(4):
+    for f in ORDER:
         multiply(f)
         if f == 0:
             pl.semaphore_wait(barrier, greeted)
         first_ahead(0, f)
-    for f in range(4):
         first_back(0, f)
+    first_relay(0)
+    for f in ORDER:
+        first_ahead(1, f)
     for copy in inputs[2:]:
         copy.wait()
     ref32[...] = ref[...].astype(F32)
@@ -501,49 +489,32 @@
         + jnp.where(lane_all == 1, kl_col, 0.0)
         + jnp.where(lane_all == 2, target_col, 0.0)
     )
-    first_relay(0)
-    for f in range(4):
-        first_ahead(1, f)
-    for f in range(4):
+    first_sum(0)
+    for f in ORDER:
         first_back(1, f)
     ref_side = [ref_stats(0), ref_stats(1)]
+    first_relay(1)
+    second_sum(0)
+    stats_send(0, ref_side[0])
+    first_sum(1)
+    gradients(0, *stats_finish(0))
+    second_sum(1)
+    stats_send(1, ref_side[1])
+    ag_pass(0, (0, 1, 2), (3, 4))
+    gradients(1, *stats_finish(1))
+    ag_pass(0, (3,), (5,))
+    ag_pass(1, (0, 1, 2), (3, 4))
+    tokens_go(1)
     for g in range(GROUPS):
         rows_turned[:, g * members : (g + 1) * members] = lax.dot_general(
             hidden[...], spread(g), (((0,), (0,)), ((), ())), preferred_element_type=F32
         ).astype(BF16)
     rows_copy = pltpu.make_async_copy(rows_turned, rows_out, end_sem.at[0])
     rows_copy.start()
-    first_sum(0)
-    first_relay(1)
-    second_relay(0)
-    first_sum(1)
-    second_sum(0)
-    stats_send(0, ref_side[0])
-    second_relay(1)
-    gradients(0, *stats_finish(0))
-    ag_go(0, (0, 1))
-    second_sum(1)
-    stats_send(1, ref_side[1])
-    ag_arrived(0, (0,))
-    ag_go(0, (2,))
-    gradients(1, *stats_finish(1))
-    ag_go(1, (0, 1))
-    tokens_go(1)
-    ag_arrived(0, (1, 2))
-    ag_go(0, (3, 4))
-    ag_arrived(1, (0,))
-    ag_go(1, (2,))
-    ag_arrived(1, (1, 2))
-    ag_go(1, (3, 4))
-    ag_arrived(0, (3,))
-    ag_go(0, (5,))
-    ag_arrived(1, (3,))
-    ag_go(1, (5,))
+    ag_pass(1, (3,), (5,))
     tokens_moved(1, tk_recv)
     tokens_go(0)
-    ag_arrived(0, (4, 5))
     slots[...] = feature_step(0)
-    ag_arrived(1, (4, 5))
     slots[...] = slots[...] + feature_step(1)
 
     core_copy = pltpu.make_async_remote_copy(
@@ -664,13 +635,14 @@
     for f in range(4):
         load(f).wait()
         for h in range(2):
-            total = 0.0
-            for g in range(GROUPS):
-                piece = grads[f, g, :, :, h * ROWS : (h + 1) * ROWS, :].reshape(members, width)
-                total = total + jnp.dot(
-                    rows[:, g * members : (g + 1) * members], piece, preferred_element_type=F32
-                )
-            result[f, h] = total.astype(BF16)
+            block = jnp.concatenate(
+                [
+                    grads[f, g, :, :, h * ROWS : (h + 1) * ROWS, :].reshape(members, width)
+                    for g in range(GROUPS)
+                ],
+                axis=0,
+            )
+            result[f, h] = jnp.dot(rows[...], block, preferred_element_type=F32).astype(BF16)
             store(f, h).start()
     tokens_copy.wait()
     outs = []
@@ -745,9 +717,9 @@
             pltpu.SemaphoreType.DMA((6,)),
             pltpu.SemaphoreType.DMA((4,)),
             pltpu.SemaphoreType.DMA((GROUPS, 2)),
-            pltpu.SemaphoreType.DMA((GROUPS, 6)),
+            pltpu.SemaphoreType.DMA((GROUPS, 6, 4)),
             pltpu.SemaphoreType.DMA((GROUPS, 2)),
-            pltpu.SemaphoreType.DMA((GROUPS, 6)),
+            pltpu.SemaphoreType.DMA((GROUPS, 6, 4)),
             pltpu.SemaphoreType.DMA((GROUPS,)),
             pltpu.SemaphoreType.DMA((GROUPS,)),
             pltpu.SemaphoreType.DMA((2,)),

time: 88.3 us -> 82.8 us (0.938)
  Pallas kernels: 87.4 us -> 81.9 us
    pallas_call x1, Pallas kernels: 79.9 us -> 76.6 us  [per_device(): pl.pallas_call(functools.partial(head_kernel, vocab_count), out_shape=(ja...]
    pallas_call x1, Pallas kernels: 7.55 us -> 5.35 us  [per_device(): pl.pallas_call(weight_kernel, out_shape=(jax.ShapeDtypeStruct((depth, col...]
where the time goes in v1:
time: 82.8 us; the launch traced here: 82.7 us
  Pallas kernels  81.9 us (99%)
    pallas_call x1, Pallas kernels, per_device(): pl.pallas_call(functools.partial(head_kernel, vocab_count), out_shape=(ja...  76.6 us
    pallas_call x1, Pallas kernels, per_device(): pl.pallas_call(weight_kernel, out_shape=(jax.ShapeDtypeStruct((depth, col...  5.35 us

profile of v1, /device:TPU:1, one launch (start us, length us, event | category | flops | bytes accessed | tf_op | source)
XLA Modules:
  0.0 82.7 jit_solution(2202520879681544326)
XLA Ops:
  0.6 76.6 %head.1 = (bf16[2,4,4,4,16,1024]{5,4,3,2,1,0:T(8,128)(2,1)}, bf16[512,256]{1,0:T(8,128)(2,1)}, bf16[64,512]{1,0:T(8,128)(2,1)}, f32[8,128]{1,0:T(8,128)}) custom-call(bf16[512,512]{1,0:T(8,128)(2,1)} %hidden_hbm.1, bf16[512,8192]{1,0:T(8,128)(2,1)} %weight_hbm.1, bf16[16,8192]{1,0:T(8,128)(2,1)} %ref_hbm.1, s32[1,256]{1,0:T(1,128)} %bitcast.9, ...), custom_call_target="tpu_custom_call" | custom-call | flops 4294967296 | bytes 12582912 | tf_op jit(solution)/shard_map/head/pallas_call | solution.py:679
  77.2 5.3 %weight_grad.1 = (bf16[512,8192]{1,0:T(8,128)(2,1)}, bf16[64,512]{1,0:T(8,128)(2,1)}, f32[1,32]{1,0:T(1,128)}, f32[1,32]{1,0:T(1,128)}, f32[1,32]{1,0:T(1,128)}) custom-call(bf16[512,256]{1,0:T(8,128)(2,1)} %get-tuple-element.14.rows_in, bf16[2,4,4,4,16,1024]{5,4,3,2,1,0:T(8,128)(2,1)} %get-tuple-element.15.grads_in, ...), custom_call_target="tpu_custom_call" | custom-call | flops 2147483648 | bytes 12582912 | tf_op jit(solution)/shard_map/weight_grad/pallas_call | solution.py:751

commit v2 on v1

--- a/solution.py
+++ b/solution.py
@@ -90,6 +90,7 @@
     stats,
     tokens,
     slots,
+    spreads,
     ref32,
     core_recv,
     zsend,
@@ -162,7 +163,7 @@
         cols = pl.ds(f * width, width)
         return pltpu.make_async_copy(weight_hbm.at[:, cols], weight.at[f], w_sem.at[f])
 
-    for f in range(4):
+    for f in ORDER:
         weight_copy(f).start()
 
     def iota(shape, dim):
@@ -458,15 +459,17 @@
                     (((1,), (1,)), ((), ())),
                     preferred_element_type=F32,
                 )
-        to_slots = spread(g)
         high = total.astype(BF16)
         rest = total - high.astype(F32)
         middle = rest.astype(BF16)
         low = (rest - middle.astype(F32)).astype(BF16)
-        placed = jnp.dot(to_slots, high, preferred_element_type=F32)
-        placed = placed + jnp.dot(to_slots, middle, preferred_element_type=F32)
-        placed = placed + jnp.dot(to_slots, low, preferred_element_type=F32)
-        return placed.reshape(slots.shape)
+        return high, middle, low
+
+    def placed(g, l, split):
+        total = 0.0
+        for piece in split:
+            total = total + jnp.dot(spreads[g, l], piece, preferred_element_type=F32)
+        return total.reshape(slots.shape[1:])
 
     for f in ORDER:
         multiply(f)
@@ -506,43 +509,42 @@
     ag_pass(1, (0, 1, 2), (3, 4))
     tokens_go(1)
     for g in range(GROUPS):
+        to_slots = spread(g)
+        spreads[g] = to_slots.reshape(spreads.shape[1:])
         rows_turned[:, g * members : (g + 1) * members] = lax.dot_general(
-            hidden[...], spread(g), (((0,), (0,)), ((), ())), preferred_element_type=F32
+            hidden[...], to_slots, (((0,), (0,)), ((), ())), preferred_element_type=F32
         ).astype(BF16)
     rows_copy = pltpu.make_async_copy(rows_turned, rows_out, end_sem.at[0])
     rows_copy.start()
     ag_pass(1, (3,), (5,))
     tokens_moved(1, tk_recv)
     tokens_go(0)
-    slots[...] = feature_step(0)
-    slots[...] = slots[...] + feature_step(1)
-
-    core_copy = pltpu.make_async_remote_copy(
-        src_ref=slots.at[:, 1 - core],
-        dst_ref=core_recv,
-        send_sem=core_send_sem,
-        recv_sem=core_recv_sem,
-        device_id=(dp, level * 2 + 1 - core),
-        device_id_type=MESH,
-    )
-    core_copy.start()
-
-    tokens_moved(0, tk_recv)
-    everyone = tokens[...].reshape(count, LANES)
-    mine_slots = slot_col == dp * slot_count + lane_all
-    mine_slots = mine_slots & (lane_all < slot_count)
-    for k in range(3):
-        tokens_result[k : k + 1, :] = jnp.sum(
-            jnp.where(mine_slots, everyone[:, k : k + 1], 0.0), axis=0, keepdims=True
-        )
-
-    tokens_copied = pltpu.make_async_copy(tokens_result, tokens_out, end_sem.at[1])
-    tokens_copied.start()
-    core_copy.wait_recv()
+    split = feature_step(0)
+    for l in range(levels):
+        slots[l] = placed(0, l, split)
+
+    def core_copy(l):
+        return pltpu.make_async_remote_copy(
+            src_ref=slots.at[l, 1 - core],
+            dst_ref=core_recv.at[l],
+            send_sem=core_send_sem.at[l],
+            recv_sem=core_recv_sem.at[l],
+            device_id=(dp, level * 2 + 1 - core),
+            device_id_type=MESH,
+        )
+
+    turns = [step for step in (2, 1, 3, 0) if step < levels]
+    split = feature_step(1)
+    for step in turns:
+        l = lax.rem(level + step, levels)
+        slots[l] = slots[l] + placed(1, l, split)
+        core_copy(l).start()
+
     slot_rows = slots.shape[2]
     feature_width = slots.shape[3]
 
     def pair_sum(l):
+        core_copy(l).wait_recv()
         return slots[l, core] + core_recv[l]
 
     def z_copy(step):
@@ -555,11 +557,22 @@
             device_id_type=MESH,
         )
 
-    for step in (2, 1, 3):
-        if step < levels:
-            both = pair_sum((level + step) % levels)
+    for step in turns:
+        if step > 0:
+            both = pair_sum(lax.rem(level + step, levels))
             encode([both[k : k + ROWS] for k in range(0, slot_rows, ROWS)], zsend.at[step])
             z_copy(step).start()
+    tokens_moved(0, tk_recv)
+    everyone = tokens[...].reshape(count, LANES)
+    mine_slots = slot_col == dp * slot_count + lane_all
+    mine_slots = mine_slots & (lane_all < slot_count)
+    for k in range(3):
+        tokens_result[k : k + 1, :] = jnp.sum(
+            jnp.where(mine_slots, everyone[:, k : k + 1], 0.0), axis=0, keepdims=True
+        )
+
+    tokens_copied = pltpu.make_async_copy(tokens_result, tokens_out, end_sem.at[1])
+    tokens_copied.start()
     total = pair_sum(level)
     for step in range(1, levels):
         z_copy(step).wait_recv()
@@ -587,7 +600,8 @@
         left(other_stats(g), st_send.at[g])
     for axis in range(2):
         tokens_moved(axis, tk_send)
-    core_copy.wait_send()
+    for l in range(levels):
+        core_copy(l).wait_send()
     for step in range(1, levels):
         z_copy(step).wait_send()
     rows_copy.wait()
@@ -710,6 +724,7 @@
             pltpu.VMEM((GROUPS, vocab_count, ROWS, LANES), F32),
             pltpu.VMEM((SIDE, SIDE, rows_dev, LANES), F32),
             pltpu.VMEM((levels, 2, slot_rows, depth), F32),
+            pltpu.VMEM((GROUPS, levels, all_slots // levels, count // GROUPS), BF16),
             pltpu.VMEM((rows_dev, cols), F32),
             pltpu.VMEM((levels, slot_rows, depth), F32),
             pltpu.VMEM(unit3, I32),
@@ -724,8 +739,8 @@
             pltpu.SemaphoreType.DMA((GROUPS,)),
             pltpu.SemaphoreType.DMA((2,)),
             pltpu.SemaphoreType.DMA((2,)),
-            pltpu.SemaphoreType.DMA,
-            pltpu.SemaphoreType.DMA,
+            pltpu.SemaphoreType.DMA((levels,)),
+            pltpu.SemaphoreType.DMA((levels,)),
             pltpu.SemaphoreType.DMA((levels,)),
             pltpu.SemaphoreType.DMA((levels,)),
             pltpu.SemaphoreType.DMA((GROUPS, 4)),

time: 82.8 us -> 81.4 us (0.983)
  Pallas kernels: 81.9 us -> 80.5 us
    pallas_call x1, Pallas kernels: 76.6 us -> 75.1 us  [per_device(): pl.pallas_call(functools.partial(head_kernel, vocab_count), out_shape=(ja...]
where the time goes in v2:
time: 81.4 us; the launch traced here: 81.3 us
  Pallas kernels  80.5 us (99%)
    pallas_call x1, Pallas kernels, per_device(): pl.pallas_call(functools.partial(head_kernel, vocab_count), out_shape=(ja...  75.1 us
    pallas_call x1, Pallas kernels, per_device(): pl.pallas_call(weight_kernel, out_shape=(jax.ShapeDtypeStruct((depth, col...  5.35 us

profile of v2, /device:TPU:1, one launch (start us, length us, event | category | flops | bytes accessed | tf_op | source)
XLA Modules:
  0.0 81.3 jit_solution(16567577447524874566)
XLA Ops:
  0.6 75.1 %head.1 = (bf16[2,4,4,4,16,1024]{5,4,3,2,1,0:T(8,128)(2,1)}, bf16[512,256]{1,0:T(8,128)(2,1)}, bf16[64,512]{1,0:T(8,128)(2,1)}, f32[8,128]{1,0:T(8,128)}) custom-call(bf16[512,512]{1,0:T(8,128)(2,1)} %hidden_hbm.1, bf16[512,8192]{1,0:T(8,128)(2,1)} %weight_hbm.1, bf16[16,8192]{1,0:T(8,128)(2,1)} %ref_hbm.1, s32[1,256]{1,0:T(1,128)} %bitcast.9, ...), custom_call_target="tpu_custom_call" | custom-call | flops 4294967296 | bytes 12582912 | tf_op jit(solution)/shard_map/head/pallas_call | solution.py:693
  75.8 5.3 %weight_grad.1 = (bf16[512,8192]{1,0:T(8,128)(2,1)}, bf16[64,512]{1,0:T(8,128)(2,1)}, f32[1,32]{1,0:T(1,128)}, f32[1,32]{1,0:T(1,128)}, f32[1,32]{1,0:T(1,128)}) custom-call(bf16[512,256]{1,0:T(8,128)(2,1)} %get-tuple-element.14.rows_in, bf16[2,4,4,4,16,1024]{5,4,3,2,1,0:T(8,128)(2,1)} %get-tuple-element.15.grads_in, ...), custom_call_target="tpu_custom_call" | custom-call | flops 2147483648 | bytes 12582912 | tf_op jit(solution)/shard_map/weight_grad/pallas_call | solution.py:766

commit v3 on v2

--- a/solution.py
+++ b/solution.py
@@ -377,6 +377,8 @@
             grads[s, f, here[0], here[1]] = result.astype(BF16)
             for kind in (0, 1, 2):
                 ag_copy(s, f, kind).start()
+            if s == 0:
+                line_go(f, 0)
 
     def relay_copy(buffer, f, kind, straight, send_sem, recv_sem):
         axis, way = FLOWS[f]
@@ -402,6 +404,19 @@
         return relay_copy(
             grads.at[g, f], f, kind, True, ag_send.at[g, kind // 3], ag_recv.at[g, kind, f]
         )
+
+    def line_go(f, offset):
+        axis, way = FLOWS[f]
+        block = grads.at[(0, f) + place(f, along(axis, offset), here[1 - axis])]
+        for kind, to in ((3, way), (4, -way)):
+            pltpu.make_async_remote_copy(
+                src_ref=block,
+                dst_ref=block,
+                send_sem=ag_send.at[0, 1],
+                recv_sem=ag_recv.at[0, kind, f],
+                device_id=device(1 - axis, to),
+                device_id_type=MESH,
+            ).start()
 
     def ag_pass(g, waits, kinds):
         for f in ORDER:
@@ -503,7 +518,10 @@
     gradients(0, *stats_finish(0))
     second_sum(1)
     stats_send(1, ref_side[1])
-    ag_pass(0, (0, 1, 2), (3, 4))
+    for kind in (0, 1, 2):
+        for f in ORDER:
+            ag_copy(0, f, kind).wait_recv()
+            line_go(f, (-FLOWS[f][1], FLOWS[f][1], 2)[kind])
     gradients(1, *stats_finish(1))
     ag_pass(0, (3,), (5,))
     ag_pass(1, (0, 1, 2), (3, 4))

time: 81.4 us -> 80.4 us (0.988)
  Pallas kernels: 80.5 us -> 79.5 us
    pallas_call x1, Pallas kernels: 75.1 us -> 74.2 us  [per_device(): pl.pallas_call(functools.partial(head_kernel, vocab_count), out_shape=(ja...]
where the time goes in v3:
time: 80.4 us; the launch traced here: 80.3 us
  Pallas kernels  79.5 us (99%)
    pallas_call x1, Pallas kernels, per_device(): pl.pallas_call(functools.partial(head_kernel, vocab_count), out_shape=(ja...  74.2 us
    pallas_call x1, Pallas kernels, per_device(): pl.pallas_call(weight_kernel, out_shape=(jax.ShapeDtypeStruct((depth, col...  5.35 us

profile of v3, /device:TPU:1, one launch (start us, length us, event | category | flops | bytes accessed | tf_op | source)
XLA Modules:
  0.0 80.3 jit_solution(3419389076317172191)
XLA Ops:
  0.6 74.2 %head.1 = (bf16[2,4,4,4,16,1024]{5,4,3,2,1,0:T(8,128)(2,1)}, bf16[512,256]{1,0:T(8,128)(2,1)}, bf16[64,512]{1,0:T(8,128)(2,1)}, f32[8,128]{1,0:T(8,128)}) custom-call(bf16[512,512]{1,0:T(8,128)(2,1)} %hidden_hbm.1, bf16[512,8192]{1,0:T(8,128)(2,1)} %weight_hbm.1, bf16[16,8192]{1,0:T(8,128)(2,1)} %ref_hbm.1, s32[1,256]{1,0:T(1,128)} %bitcast.9, ...), custom_call_target="tpu_custom_call" | custom-call | flops 4294967296 | bytes 12582912 | tf_op jit(solution)/shard_map/head/pallas_call | solution.py:711
  74.8 5.3 %weight_grad.1 = (bf16[512,8192]{1,0:T(8,128)(2,1)}, bf16[64,512]{1,0:T(8,128)(2,1)}, f32[1,32]{1,0:T(1,128)}, f32[1,32]{1,0:T(1,128)}, f32[1,32]{1,0:T(1,128)}) custom-call(bf16[512,256]{1,0:T(8,128)(2,1)} %get-tuple-element.14.rows_in, bf16[2,4,4,4,16,1024]{5,4,3,2,1,0:T(8,128)(2,1)} %get-tuple-element.15.grads_in, ...), custom_call_target="tpu_custom_call" | custom-call | flops 2147483648 | bytes 12582912 | tf_op jit(solution)/shard_map/weight_grad/pallas_call | solution.py:784

commit v4 on v2

--- a/solution.py
+++ b/solution.py
@@ -377,6 +377,7 @@
             grads[s, f, here[0], here[1]] = result.astype(BF16)
             for kind in (0, 1, 2):
                 ag_copy(s, f, kind).start()
+            line_go(s, f, 0)
 
     def relay_copy(buffer, f, kind, straight, send_sem, recv_sem):
         axis, way = FLOWS[f]
@@ -402,6 +403,25 @@
         return relay_copy(
             grads.at[g, f], f, kind, True, ag_send.at[g, kind // 3], ag_recv.at[g, kind, f]
         )
+
+    def line_go(g, f, offset):
+        axis, way = FLOWS[f]
+        block = grads.at[(g, f) + place(f, along(axis, offset), here[1 - axis])]
+        for kind, to in ((3, way), (4, -way)):
+            pltpu.make_async_remote_copy(
+                src_ref=block,
+                dst_ref=block,
+                send_sem=ag_send.at[g, 1],
+                recv_sem=ag_recv.at[g, kind, f],
+                device_id=device(1 - axis, to),
+                device_id_type=MESH,
+            ).start()
+
+    def line_pass(g):
+        for kind in (0, 1, 2):
+            for f in ORDER:
+                ag_copy(g, f, kind).wait_recv()
+                line_go(g, f, (-FLOWS[f][1], FLOWS[f][1], 2)[kind])
 
     def ag_pass(g, waits, kinds):
         for f in ORDER:
@@ -503,10 +523,10 @@
     gradients(0, *stats_finish(0))
     second_sum(1)
     stats_send(1, ref_side[1])
-    ag_pass(0, (0, 1, 2), (3, 4))
+    line_pass(0)
     gradients(1, *stats_finish(1))
     ag_pass(0, (3,), (5,))
-    ag_pass(1, (0, 1, 2), (3, 4))
+    line_pass(1)
     tokens_go(1)
     for g in range(GROUPS):
         to_slots = spread(g)

time: 81.4 us -> 79.6 us (0.978)
  Pallas kernels: 80.5 us -> 78.7 us
    pallas_call x1, Pallas kernels: 75.1 us -> 73.3 us  [per_device(): pl.pallas_call(functools.partial(head_kernel, vocab_count), out_shape=(ja...]
where the time goes in v4:
time: 79.6 us; the launch traced here: 79.5 us
  Pallas kernels  78.7 us (99%)
  between operations  0.8 us (1%)
    pallas_call x1, Pallas kernels, per_device(): pl.pallas_call(functools.partial(head_kernel, vocab_count), out_shape=(ja...  73.3 us
    pallas_call x1, Pallas kernels, per_device(): pl.pallas_call(weight_kernel, out_shape=(jax.ShapeDtypeStruct((depth, col...  5.35 us

profile of v4, /device:TPU:1, one launch (start us, length us, event | category | flops | bytes accessed | tf_op | source)
XLA Modules:
  0.0 79.5 jit_solution(12008919265161930512)
XLA Ops:
  0.6 73.3 %head.1 = (bf16[2,4,4,4,16,1024]{5,4,3,2,1,0:T(8,128)(2,1)}, bf16[512,256]{1,0:T(8,128)(2,1)}, bf16[64,512]{1,0:T(8,128)(2,1)}, f32[8,128]{1,0:T(8,128)}) custom-call(bf16[512,512]{1,0:T(8,128)(2,1)} %hidden_hbm.1, bf16[512,8192]{1,0:T(8,128)(2,1)} %weight_hbm.1, bf16[16,8192]{1,0:T(8,128)(2,1)} %ref_hbm.1, s32[1,256]{1,0:T(1,128)} %bitcast.9, ...), custom_call_target="tpu_custom_call" | custom-call | flops 4294967296 | bytes 12582912 | tf_op jit(solution)/shard_map/head/pallas_call | solution.py:713
  74.0 5.3 %weight_grad.1 = (bf16[512,8192]{1,0:T(8,128)(2,1)}, bf16[64,512]{1,0:T(8,128)(2,1)}, f32[1,32]{1,0:T(1,128)}, f32[1,32]{1,0:T(1,128)}, f32[1,32]{1,0:T(1,128)}) custom-call(bf16[512,256]{1,0:T(8,128)(2,1)} %get-tuple-element.14.rows_in, bf16[2,4,4,4,16,1024]{5,4,3,2,1,0:T(8,128)(2,1)} %get-tuple-element.15.grads_in, ...), custom_call_target="tpu_custom_call" | custom-call | flops 2147483648 | bytes 12582912 | tf_op jit(solution)/shard_map/weight_grad/pallas_call | solution.py:786
